TPU v7x, 256 devices: a whole 4x4x8 slice. The times are simulated.
256 devices in a mesh: sec: 4 (over y_lo, core), tile: 64 (over z, y_hi, x).
Axes of the slice: x: 4, y: 4 (y_hi: 2, y_lo: 2; y = y_hi * 2 + y_lo), z: 8, core: 2. Of those that a mesh axis runs over, the one named last changes fastest.
Arguments:
- surface: float32 [4, 4096, 2560], P('sec', 'tile'), may hold values from -6 to 6
- remap_weights: float32 [4096, 8, 4096], P('tile'), may hold values from -0.25 to 0.25
- src_tiles: int32 [4096, 8], P('tile'), may hold values from 0 to 12287, as said below
- block_count: int32 [4096], P('tile'), may hold values from 1 to 8, as said below
- land_sea: int32 [4096, 64], P('tile'), may hold values from 0 to 1
- exchange_coef: float32 [40], replicated, may hold values from 0.2 to 2
Outputs:
- section_flux: float32 [4, 4096, 2560], P('sec', 'tile')
Inputs may be any that keep to these rules, and one draw needn't show every extreme that they name: `src_tiles`: every id names an atmosphere tile whose band (id mod 4096) // 64 lies within one band, cyclically, of the ocean tile's band t // 64; ids at k >= block_count[t] are ignored. `block_count`: some tile has 8 blocks.
All inputs are finite; a program needn't handle non-finite values.
Results may differ from a plain program's by a relative error of at most 0.0001.
Values sent between devices are 32-bit elements; how exact they have to be, the bound alone decides.
A program may use at most 128 MiB of HBM per device.

v0:
```python
import jax
import jax.numpy as jnp
from jax import lax
from jax.sharding import PartitionSpec as P


def extended_2(array, sides, width):
    for axis, dim in sides:
        devices, length = (lax.axis_size(axis), array.shape[dim])
        up = [(i, (i + 1) % devices) for i in range(devices)]
        down = [(j, i) for i, j in up]
        last = lax.slice_in_dim(array, length - width, length, axis=dim)
        leading = lax.slice_in_dim(array, 0, width, axis=dim)
        before = lax.ppermute(last, axis, up)
        after = lax.ppermute(leading, axis, down)
        array = jnp.concatenate([before, array, after], axis=dim)
    return array


def spread(array, axis, root):
    mine = lax.axis_index(axis) == root
    return lax.psum(jnp.where(mine, array, jnp.zeros_like(array)), axis)


def from_behind(block, axis, distance):
    devices = range(lax.axis_size(axis))
    route = [((i - distance) % len(devices), i) for i in devices]
    return lax.ppermute(block, axis, route)


def on_device(surface, remap_weights, src_tiles, block_count, land_sea, exchange_coef):
    tile_dev = surface.shape[1]
    wide = surface.shape[2]
    fields = exchange_coef.shape[0]
    cells = wide // fields
    blocks = src_tiles.shape[1]
    bands = lax.axis_size("tile")
    sections = lax.axis_size("sec")
    sec_tiles = bands * tile_dev
    band = lax.axis_index("tile")
    section = lax.axis_index("sec")
    weights = remap_weights.reshape(tile_dev, blocks, cells, cells)
    valid = jnp.arange(blocks)[None, :] < block_count[:, None]
    source_sec = src_tiles // sec_tiles
    within = src_tiles % sec_tiles
    offset = (within // tile_dev - band + 1 + bands) % bands
    local_row = offset * tile_dev + within % tile_dev
    mine = valid & (source_sec == section)
    own_band = surface[0].reshape(tile_dev, fields, cells)
    every = lax.all_gather(surface, "sec", axis=0, tiled=True)
    extended = extended_2(every, (("tile", 1),), tile_dev)
    rows = extended.reshape(sections * 3 * tile_dev, wide)
    picked = rows[source_sec * 3 * tile_dev + local_row]
    picked = jnp.where(valid[:, :, None], picked, 0.0).reshape(tile_dev, blocks, fields, cells)
    remapped = jnp.einsum("tkfc,tkcd->tfd", picked, weights, precision=lax.Precision.HIGHEST)
    rel = remapped - own_band
    speed = jnp.sqrt(rel[:, 0] * rel[:, 0] + rel[:, 1] * rel[:, 1] + 0.25)
    stab = 1.0 + 0.5 * jnp.tanh(-rel[:, 2])
    land = land_sea.astype(jnp.float32)
    flux = (exchange_coef[None, :, None] * (speed * stab * land)[:, None, :] * rel).reshape(
        tile_dev, wide
    )
    shared = spread(flux, "sec", sections - 1)
    shared_flux = shared.reshape(tile_dev, fields, cells)
    contrib = jnp.einsum("tfd,tkcd->tkfc", shared_flux, weights, precision=lax.Precision.HIGHEST)
    contrib = jnp.where(mine[:, :, None, None], contrib, 0.0).reshape(tile_dev * blocks, wide)
    totals = jnp.zeros((3 * tile_dev, wide), jnp.float32).at[local_row.reshape(-1)].add(contrib)
    from_east = from_behind(totals[:tile_dev], "tile", -1)
    from_west = from_behind(totals[2 * tile_dev :], "tile", 1)
    back = totals[tile_dev : 2 * tile_dev] + from_east + from_west
    result = jnp.where(section == sections - 1, shared, back)
    return result[None]


def solution(mesh):
    placed = (
        P("sec", "tile", None),
        P("tile", None, None),
        P("tile", None),
        P("tile"),
        P("tile", None),
        P(),
    )
    return jax.shard_map(
        on_device, mesh=mesh, in_specs=placed, out_specs=P("sec", "tile", None), check_vma=False
    )
```

profile of v0, /device:TPU:1, one launch (start us, length us, event | category | flops | bytes accessed | tf_op | source)
XLA Modules:
  0.0 313.6 jit_solution(6457273414330569962)
XLA Ops:
  6.5 0.7 all-gather.2.cloned.1.call-update
  7.3 42.1 %all-gather.2.cloned.1.call-done = f32[4,64,2560]{2,1,0:T(8,128)} async-done(((f32[1,64,2560]{2,1,0:T(8,128)}), f32[4,64,2560]{2,1,0:T(8,128)}) %all-gather.2.cloned.1.call-update) | async-done | bytes 2621456 | tf_op jit(solution)/shard_map/all_gather | solution.py:50
  49.4 1.2 collective-permute-start
  50.6 6.1 %collective-permute-start.1 = (f32[4,64,2560]{2,1,0:T(8,128)}, f32[4,64,2560]{2,1,0:T(8,128)}, u32[]{:S(2)}, u32[]{:S(2)}) collective-permute-start(f32[4,64,2560]{2,1,0:T(8,128)} %all-gather.2.cloned.1.call-done), channel_id=1, source_target_pairs={{1,0},{2,1},{3,2},{4,3},{5,4},{6,5},{7,6},{8,7},{9,8},{10,9},{11,1... | collective-permute-start | bytes 7864328 | tf_op jit(solution)/shard_map/ppermute | solution.py:15
  56.8 1.4 reshape_squeeze.3
  58.5 14.2 %reshape.86 = f32[64,8,64,64]{3,2,1,0:T(8,128)} reshape(f32[64,8,4096]{2,1,0:T(8,128)} %param.7) | data formatting | bytes 16777216 | tf_op jit(solution)/shard_map/reshape | solution.py:42
  72.7 41.5 %collective-permute-done = f32[4,64,2560]{2,1,0:T(8,128)} collective-permute-done((f32[4,64,2560]{2,1,0:T(8,128)}, f32[4,64,2560]{2,1,0:T(8,128)}, u32[]{:S(2)}, u32[]{:S(2)}) %collective-permute-start) | collective-permute-done | bytes 2621472 | tf_op jit(solution)/shard_map/ppermute | solution.py:14
  114.2 5.4 %pad_maximum_fusion = f32[4,192,2560]{2,1,0:T(8,128)} fusion(f32[4,64,2560]{2,1,0:T(8,128)} %collective-permute-done.1, f32[4,64,2560]{2,1,0:T(8,128)} %all-gather.2.cloned.1.call-done, f32[4,64,2560]{2,1,0:T(8,128)} %collective-permute-done), kind=kLoop, calls=%fused_computation.5 | loop fusion | flops 3932160 | bytes 15728640 | tf_op jit(solution)/shard_map/concatenate | solution.py:16
  119.6 9.5 %gather_fusion = f32[512,2560]{1,0:T(8,128)} fusion(f32[768,2560]{1,0:T(8,128)} %bitcast.20, s32[1024]{0:T(1024)S(1)} %pad_clamp_fusion), kind=kCustom, calls=%fused_computation | custom fusion | bytes 10487808 | tf_op jit(solution)/shard_map/gather | solution.py:53
  129.1 8.7 %gather.6 = f32[64,8,40,64]{3,2,1,0:T(8,128)} reshape(f32[512,2560]{1,0:T(8,128)} %gather_fusion) | data formatting | bytes 10485760 | tf_op jit(solution)/shard_map/gather | solution.py:53
  137.8 16.7 %fusion.4 = f32[64,40,64]{2,1,0:T(8,128)S(1)} fusion(f32[64,8,64,64]{3,2,1,0:T(8,128)} %reshape.86, f32[64,8,40,64]{3,2,1,0:T(8,128)} %gather.6, pred[64,8]{1,0:T(8,128)(4,1)S(1)} %copy.22), kind=kOutput, calls=%fused_computation.8 | convolution fusion | flops 1007943680 | bytes 14287360 | tf_op jit(solution)/shard_map/tkfc,tkcd->tfd/dot_general | solution.py:55
  154.5 0.4 copy_subtract_fusion
  155.0 0.3 copy-done.1
  155.5 0.8 copy.26
  156.3 1.2 select_n.75
  157.8 44.8 %all-reduce.2.cloned.1.call-done = f32[64,2560]{1,0:T(8,128)} async-done(((f32[64,2560]{1,0:T(8,128)}), f32[64,2560]{1,0:T(8,128)}) %all-reduce.2.cloned.1.call-update) | async-done | bytes 655376 | tf_op jit(solution)/shard_map/psum | solution.py:22
  202.6 1.4 reshape.111
  204.0 52.5 %select_bitcast_fusion = f32[64,8,40,64]{3,2,1,0:T(8,128)} fusion(pred[64,8]{1,0:T(8,128)(4,1)S(1)} %copy.28, f32[64,8,64,64]{3,2,1,0:T(8,128)} %reshape.86, f32[64,40,64,1]{2,1,0,3:T(8,128)S(1)} %reshape.111), kind=kOutput, calls=%fused_computation.2 | convolution fusion | flops 1007943680 | bytes 14287360 | tf_op jit(solution)/shard_map/tfd,tkcd->tkfc/dot_general | solution.py:65
  256.4 9.6 %reshape.103 = f32[512,2560]{1,0:T(8,128)} reshape(f32[64,8,40,64]{3,2,1,0:T(8,128)} %select_bitcast_fusion) | data formatting | bytes 10485760 | tf_op jit(solution)/shard_map/reshape | solution.py:66
  266.0 10.6 %scatter_custom_fusion = f32[192,2560]{1,0:T(8,128)S(1)} fusion(s32[512]{0:T(512)S(1)} %bitcast.21, f32[512,2560]{1,0:T(8,128)} %reshape.103, f32[]{:T(128)} %constant.82.clone.1), kind=kCustom, calls=%fused_computation.12 | custom fusion | flops 1310720 | bytes 1966592 | tf_op jit(solution)/shard_map/scatter-add | solution.py:67
  276.7 7.4 %collective-permute-start.2 = (f32[64,2560]{1,0:T(8,128)S(1)}, f32[64,2560]{1,0:T(8,128)S(1)}, u32[]{:S(2)}, u32[]{:S(2)}) collective-permute-start(f32[64,2560]{1,0:T(8,128)S(1)} %get-tuple-element.7), channel_id=1, source_target_pairs={{1,0},{2,1},{3,2},{4,3},{5,4},{6,5},{7,6},{8,7},{9,8},{10,9},{11,1... | collective-permute-start | bytes 1966088 | tf_op jit(solution)/shard_map/ppermute | solution.py:28
  284.1 14.0 %collective-permute-done.2 = f32[64,2560]{1,0:T(8,128)S(1)} collective-permute-done((f32[64,2560]{1,0:T(8,128)S(1)}, f32[64,2560]{1,0:T(8,128)S(1)}, u32[]{:S(2)}, u32[]{:S(2)}) %collective-permute-start.2) | collective-permute-done | bytes 655392 | tf_op jit(solution)/shard_map/ppermute | solution.py:28
  298.1 7.6 %collective-permute-done.3 = f32[64,2560]{1,0:T(8,128)S(1)} collective-permute-done((f32[64,2560]{1,0:T(8,128)S(1)}, f32[64,2560]{1,0:T(8,128)S(1)}, u32[]{:S(2)}, u32[]{:S(2)}) %collective-permute-start.3) | collective-permute-done | bytes 655392 | tf_op jit(solution)/shard_map/ppermute | solution.py:28
  305.7 1.0 fusion.12
  (27 shorter events, 1.0 us)
Async XLA Ops:
  6.5 51.6 %copy-start.2 = (s32[64,8]{0,1:T(8,128)S(1)}, s32[64,8]{0,1:T(8,128)}, u32[]{:S(2)}) copy-start(s32[64,8]{0,1:T(8,128)} %param.8) | copy-start | bytes 6148
  6.5 51.8 %copy-start.4 = (s32[64]{0:T(128)S(1)}, s32[64]{0:T(128)}, u32[]{:S(2)}) copy-start(s32[64]{0:T(128)} %param.9) | copy-start | bytes 772
  6.5 42.9 %all-gather.2.cloned.1.call-start = ((), (), s32[]{:S(2)}) async-start(), calls=%async_computation | async-start | bytes 3276800 | tf_op jit(solution)/shard_map/all_gather | solution.py:50
  7.3 195.3 %all-reduce.2.cloned.1.call-start = ((), (), s32[]{:S(2)}) async-start(), calls=%async_computation.1 | async-start | bytes 1310720 | tf_op jit(solution)/shard_map/psum | solution.py:22
  49.4 64.7 %collective-permute-start = (f32[4,64,2560]{2,1,0:T(8,128)}, f32[4,64,2560]{2,1,0:T(8,128)}, u32[]{:S(2)}, u32[]{:S(2)}) collective-permute-start(f32[4,64,2560]{2,1,0:T(8,128)} %all-gather.2.cloned.1.call-done), channel_id=1, source_target_pairs={{0,1},{1,2},{2,3},{3,4},{4,5},{5,6},{6,7},{7,8},{8,9},{9,10},{10,1... | collective-permute-start | bytes 7864328 | tf_op jit(solution)/shard_map/ppermute | solution.py:14
  50.6 63.5 %collective-permute-start.1 = (f32[4,64,2560]{2,1,0:T(8,128)}, f32[4,64,2560]{2,1,0:T(8,128)}, u32[]{:S(2)}, u32[]{:S(2)}) collective-permute-start(f32[4,64,2560]{2,1,0:T(8,128)} %all-gather.2.cloned.1.call-done), channel_id=1, source_target_pairs={{1,0},{2,1},{3,2},{4,3},{5,4},{6,5},{7,6},{8,7},{9,8},{10,9},{11,1... | collective-permute-start | bytes 7864328 | tf_op jit(solution)/shard_map/ppermute | solution.py:15
  154.5 0.8 copy-start.1
  154.5 0.8 copy-start.3
  266.0 39.7 %copy-start = (f32[64,2560]{1,0:T(8,128)S(1)}, f32[64,2560]{1,0:T(8,128)}, u32[]{:S(2)}) copy-start(f32[64,2560]{1,0:T(8,128)} %all-reduce.2.cloned.1.call-done) | copy-start | bytes 1966084
  276.7 21.4 %collective-permute-start.2 = (f32[64,2560]{1,0:T(8,128)S(1)}, f32[64,2560]{1,0:T(8,128)S(1)}, u32[]{:S(2)}, u32[]{:S(2)}) collective-permute-start(f32[64,2560]{1,0:T(8,128)S(1)} %get-tuple-element.7), channel_id=1, source_target_pairs={{1,0},{2,1},{3,2},{4,3},{5,4},{6,5},{7,6},{8,7},{9,8},{10,9},{11,1... | collective-permute-start | bytes 1966088 | tf_op jit(solution)/shard_map/ppermute | solution.py:28
  284.1 21.6 %collective-permute-start.3 = (f32[64,2560]{1,0:T(8,128)S(1)}, f32[64,2560]{1,0:T(8,128)S(1)}, u32[]{:S(2)}, u32[]{:S(2)}) collective-permute-start(f32[64,2560]{1,0:T(8,128)S(1)} %get-tuple-element.8), channel_id=1, source_target_pairs={{63,0},{0,1},{1,2},{2,3},{3,4},{4,5},{5,6},{6,7},{7,8},{8,9},{9,10... | collective-permute-start | bytes 1966088 | tf_op jit(solution)/shard_map/ppermute | solution.py:28
Sparse Core Ops, SparseCore 0:
  9.2 40.2 all-gather.1
  157.6 44.9 all-reduce.1
where the time goes:
time: 315 us; the launch traced here: 314 us
  waiting for transfers between devices  151 us (48%)
  matrix products  69.1 us (22%)
  local copies, waits for them, and re-layouts  47.6 us (15%)
  other arithmetic  17.7 us (6%)
  starting transfers between devices  14.7 us (5%)
  between operations  13.5 us (4%)
    dot_general x1, matrix products, on_device(): jnp.einsum('tfd,tkcd->tkfc', shared_flux, weights, precision=lax.Precisio...  52.5 us
    psum x1, waiting for transfers between devices, spread(): return lax.psum(jnp.where(mine, array, jnp.zeros_like(array)), axis)  44.8 us
    all_gather x1, waiting for transfers between devices, on_device(): every = lax.all_gather(surface, 'sec', axis=0, tiled=True)  42.1 us
    ppermute x1, waiting for transfers between devices, extended_2(): before = lax.ppermute(last, axis, up)  41.5 us
    ppermute x2, waiting for transfers between devices, from_behind(): return lax.ppermute(block, axis, route)  21.6 us
    gather x2, local copies, waits for them, and re-layouts, on_device(): picked = rows[source_sec * 3 * tile_dev + local_row]  18.2 us
    dot_general x1, matrix products, on_device(): jnp.einsum('tkfc,tkcd->tfd', picked, weights, precision=lax.Precision.HIG...  16.7 us
    reshape x1, local copies, waits for them, and re-layouts, on_device(): weights = remap_weights.reshape(tile_dev, blocks, cells, cells)  14.2 us
  transfers between devices with their start and end apart: 6, of which 5 were waited for; matrix products, arithmetic and copies ran while one was open for 5% of the time, Pallas kernels for 0%

commit v1 on v0

v1 whole, which is shorter than its diff:
```python
import functools
import jax
import jax.numpy as jnp
from jax import lax
from jax.experimental import pallas as pl
from jax.experimental.pallas import tpu as pltpu
from jax.sharding import PartitionSpec as P

MESH = pl.DeviceIdType.MESH
FIELDS, CELLS, BLOCKS, TILES = 40, 64, 8, 64
WIDE = FIELDS * CELLS
BANDS, SECS = 64, 4
KEEP = 48
GIVE = TILES - KEEP
SLOTS = 3 * KEEP
PAIRS = TILES // 2
HALF = PAIRS // 2
CHUNKS = (16, 24)
W_PARTS = 8
f32, bf16 = jnp.float32, jnp.bfloat16


def split(x):
    hi = x.astype(bf16).astype(f32)
    return hi, x - hi


def kernel(x_ref, w_ref, idx_ref, col_ref, wet_ref, coef_ref, out_ref, *scratch):
    n = len(CHUNKS)
    (wraw, wp, mix, hot, cb, fac, rel, fin) = scratch[:8]
    per = scratch[8 : 8 + 11 * n]
    (w_sem, own_sem, xs, xr, hs, hr, oss, orr, osl, s1s, s1r, ys, yr, s2s, s2r, bs, br, gs, gr) = (
        scratch[8 + 11 * n :]
    )
    band_in, part, sib, ysum, yrec, flux, oc, ocd, tot, rec, src = [
        [per[11 * i + j] for i in range(n)] for j in range(11)
    ]
    s, b = lax.axis_index("sec"), lax.axis_index("tile")
    core = lax.rem(s, 2)
    mate = s + 1 - 2 * core
    opp = lax.rem(s + 2, SECS)
    east, west = lax.rem(b + 1, BANDS), lax.rem(b + BANDS - 1, BANDS)
    taker = s == SECS - 1
    lane = lax.broadcasted_iota(jnp.int32, (1, 128), 1)
    low = lane < CELLS
    starts = [sum(CHUNKS[:i]) for i in range(n)]

    def remote(a, z, ss, rs, to):
        return pltpu.make_async_remote_copy(
            src_ref=a, dst_ref=z, send_sem=ss, recv_sem=rs, device_id=to, device_id_type=MESH
        )

    def lanes(i):
        return pl.ds(starts[i] * CELLS, CHUNKS[i] * CELLS)

    per_w = TILES // W_PARTS
    w_copy = [
        pltpu.make_async_copy(
            w_ref.at[pl.ds(i * per_w, per_w)], wraw.at[pl.ds(i * per_w, per_w)], w_sem.at[i]
        )
        for i in range(W_PARTS)
    ]
    keep_rows, give_rows = pl.ds(0, KEEP), pl.ds(KEEP, GIVE)
    own_copy = [
        pltpu.make_async_copy(x_ref.at[0, keep_rows, lanes(i)], band_in[i].at[1], own_sem.at[i])
        for i in range(n)
    ]

    def to_neighbours(i, block):
        return (
            remote(block, band_in[i].at[0], xs.at[i, 0], xr.at[i, 0], (s, east)),
            remote(block, band_in[i].at[2], xs.at[i, 1], xr.at[i, 1], (s, west)),
        )

    def hand_over(i, who):
        return remote(
            x_ref.at[0, give_rows, lanes(i)],
            band_in[i].at[1, pl.ds(pl.multiple_of(who * GIVE, GIVE), GIVE)],
            hs.at[i],
            hr.at[i, who],
            (SECS - 1, b),
        )

    def ocean_to(i, who):
        return remote(
            x_ref.at[0, pl.ds((who % 2) * 2 * HALF, 2 * HALF), lanes(i)],
            oc[i],
            oss.at[i, who],
            orr.at[i],
            (who, b),
        )

    def ocean_own(i):
        return pltpu.make_async_copy(
            x_ref.at[0, pl.ds(2 * HALF, 2 * HALF), lanes(i)], oc[i], osl.at[i]
        )

    for c in w_copy:
        c.start()

    @pl.when(jnp.logical_not(taker))
    def _():
        for i in range(n):
            own_copy[i].start()

    @pl.when(taker)
    def _():
        for i in range(n):
            ocean_own(i).start()

    barrier = pltpu.get_barrier_semaphore()
    for q in (1, 2, 3):
        pl.semaphore_signal(
            barrier, inc=1, device_id=(lax.rem(s + q, SECS), b), device_id_type=MESH
        )
    for z in (east, west):
        pl.semaphore_signal(barrier, inc=1, device_id=(s, z), device_id_type=MESH)
    pl.semaphore_wait(barrier, 5)

    @pl.when(jnp.logical_not(taker))
    def _():
        for i in range(n):
            hand_over(i, s).start()
            for c in to_neighbours(i, x_ref.at[0, keep_rows, lanes(i)]):
                c.start()

    def take_over(i):
        @pl.when(taker)
        def _():
            for who in range(SECS - 1):
                hand_over(i, who).wait_recv()
            for c in to_neighbours(i, band_in[i].at[1]):
                c.start()

    def prepare(t, _):
        for k in range(BLOCKS):
            hi, lo = split(wraw[t, pl.ds(k, CELLS // 2, stride=BLOCKS), :])
            left = jnp.where(low, hi, pltpu.roll(lo, CELLS, 1))
            right = jnp.where(low, pltpu.roll(hi, CELLS, 1), lo)
            mix[k, pl.ds(0, CELLS // 2, stride=2), :] = left
            mix[k, pl.ds(1, CELLS // 2, stride=2), :] = right
        for k in range(BLOCKS):
            wp[t, pl.ds(k * CELLS, CELLS), :] = mix[k].astype(bf16)
        return 0

    def prepare_part(i):
        w_copy[i].wait()
        lax.fori_loop(i * per_w, (i + 1) * per_w, prepare, 0)

    take_over(0)

    @pl.when(taker)
    def _():
        for i in range(n):
            for who in range(SECS - 1):
                ocean_to(i, who).start()

    for i in range(W_PARTS):
        prepare_part(i)
        if i + 1 < n:
            take_over(i + 1)

    rows = lax.broadcasted_iota(jnp.int32, (SLOTS, TILES * BLOCKS), 0)
    hot[...] = jnp.where(rows == col_ref[...], 1.0, 0.0).astype(bf16)

    def spread(view, count, F, dst, base):
        for g in range(count // 8):
            for j in range(F // 2):
                v = view[pl.ds(8 * g, 8), pl.ds(128 * j, 128)]
                r = pltpu.roll(v, CELLS, 1)
                at = (base + 8 * g) * F + 2 * j
                dst[pl.ds(at, 8, stride=F), :] = jnp.where(low, v, r)
                dst[pl.ds(at + 1, 8, stride=F), :] = jnp.where(low, r, v)

    def forward(i):
        F = CHUNKS[i]

        @pl.when(jnp.logical_not(taker))
        def _():
            own_copy[i].wait()

        src[i][SLOTS] = jnp.zeros((F, 128), f32)
        flat = src[i].reshape((SLOTS + 1) * F, 128)
        spread(band_in[i].at[1], KEEP, F, flat, KEEP)
        arrivals = to_neighbours(i, band_in[i].at[1])
        arrivals[0].wait_recv()
        spread(band_in[i].at[0], KEEP, F, flat, 0)
        arrivals[1].wait_recv()
        spread(band_in[i].at[2], KEEP, F, flat, 2 * KEEP)

        def pair(p, _):
            q = []
            for tp in range(2):
                t = 2 * p + tp
                cols = []
                for kp in range(BLOCKS // 2):
                    g0 = idx_ref[t * BLOCKS + 2 * kp]
                    g1 = idx_ref[t * BLOCKS + 2 * kp + 1]
                    cols.append(
                        jnp.where(
                            low,
                            src[i][g0],
                            src[i][g1],
                        )
                    )
                hi, lo = split(jnp.concatenate(cols, axis=1))
                lhs = jnp.concatenate([hi, lo], axis=0).astype(bf16)
                o = jnp.dot(lhs, wp[t], preferred_element_type=f32)
                q.append(o[:F] + pltpu.roll(o[:F], CELLS, 1) + o[F:])
            part[i][pl.ds(pl.multiple_of(p * F, 8), F), :] = jnp.where(
                low, q[0], pltpu.roll(q[1], CELLS, 1)
            )
            return 0

        first = (1 - core) * HALF
        lax.fori_loop(0, HALF, lambda u, c: pair(first + u, c), 0)
        sib_copy(i).start()
        lax.fori_loop(0, HALF, lambda u, c: pair(core * HALF + u, c), 0)

    def half_rows(i, which):
        size = HALF * CHUNKS[i]
        return pl.ds(pl.multiple_of(which * size, 8), size)

    def sib_copy(i):
        return remote(
            part[i].at[half_rows(i, 1 - core)], sib[i], s1s.at[i], s1r.at[i], (mate, b)
        )

    def y_copy(i):
        return remote(ysum[i], yrec[i], ys.at[i], yr.at[i], (opp, b))

    def flux_copy(i, which):
        at = flux[i].at[half_rows(i, which)]
        return remote(at, at, s2s.at[i], s2r.at[i], (mate, b))

    def reduce_chip(i):
        sib_copy(i).wait_recv()
        ysum[i][...] = part[i][half_rows(i, core), :] + sib[i][...]
        y_copy(i).start()

    def prepare_ocean(i):
        @pl.when(taker)
        def _():
            ocean_own(i).wait()

        @pl.when(jnp.logical_not(taker))
        def _():
            ocean_to(i, 0).wait_recv()

        spread(oc[i], 2 * HALF, CHUNKS[i], ocd[i], 0)

    def fluxes(i):
        F = CHUNKS[i]
        y_copy(i).wait_recv()

        def relative(u, _):
            at = pl.ds(pl.multiple_of(u * F, 8), F)
            a = ocd[i][pl.ds(pl.multiple_of(2 * u * F, 8), F), :]
            z = ocd[i][pl.ds(pl.multiple_of((2 * u + 1) * F, 8), F), :]
            rel[at, :] = ysum[i][at, :] + yrec[i][at, :] - jnp.where(low, a, z)
            return 0

        lax.fori_loop(0, HALF, relative, 0)
        if i == 0:
            r0, r1, r2 = [rel[pl.ds(f, HALF, stride=F), :] for f in range(3)]
            speed = jnp.sqrt(r0 * r0 + r1 * r1 + 0.25)
            stab = 1.0 + 0.5 * jnp.tanh(-r2)
            wet = wet_ref[pl.ds(pl.multiple_of(core * HALF, 8), HALF), :]
            fac[...] = speed * stab * wet
        coef = jnp.broadcast_to(coef_ref[pl.ds(starts[i], F), :], (F, 128))

        def scale(u, _):
            at = pl.ds(pl.multiple_of(u * F, 8), F)
            to = pl.ds(pl.multiple_of((core * HALF + u) * F, 8), F)
            flux[i][to, :] = coef * fac[pl.ds(u, 1), :] * rel[at, :]
            return 0

        lax.fori_loop(0, HALF, scale, 0)
        flux_copy(i, core).start()

    def back_copies(i):
        return (
            remote(tot[i].at[0], rec[i].at[1], bs.at[i, 0], br.at[i, 1], (s, west)),
            remote(tot[i].at[2], rec[i].at[0], bs.at[i, 1], br.at[i, 0], (s, east)),
        )

    def backward(i):
        F = CHUNKS[i]
        flux_copy(i, 1 - core).wait_recv()

        def pair(p, _):
            v = flux[i][pl.ds(pl.multiple_of(p * F, 8), F), :]
            r = pltpu.roll(v, CELLS, 1)
            for tp in range(2):
                t = 2 * p + tp
                hi, lo = split(jnp.where(low, v, r) if tp == 0 else jnp.where(low, r, v))
                lhs = jnp.concatenate([hi, lo], axis=0).astype(bf16)
                o = lax.dot_general(
                    lhs, wp[t], (((1,), (1,)), ((), ())), preferred_element_type=f32
                )
                o = o[:F] + o[F:]
                for kp in range(BLOCKS // 2):
                    at = pl.multiple_of((t * (BLOCKS // 2) + kp) * F, 8)
                    cb[pl.ds(at, F), :] = o[:, 128 * kp : 128 * kp + 128]
            return 0

        lax.fori_loop(0, PAIRS, pair, 0)

        def gather(j, _):
            count = TILES * BLOCKS // 2
            x0 = cb[pl.ds(2 * j, count, stride=F), :]
            x1 = cb[pl.ds(2 * j + 1, count, stride=F), :]
            top = jnp.where(low, x0, pltpu.roll(x1, CELLS, 1))
            bottom = jnp.where(low, pltpu.roll(x0, CELLS, 1), x1)
            hi, lo = split(jnp.concatenate([top, bottom], axis=0))
            rhs = jnp.concatenate([hi, lo], axis=1).astype(bf16)
            o = jnp.dot(hot[...], rhs, preferred_element_type=f32)
            o = o[:, :128] + o[:, 128:]
            at = pl.ds(pl.multiple_of(128 * j, 128), 128)
            for z in range(3):
                tot[i][z, :, at] = o[z * KEEP : (z + 1) * KEEP]
            return 0

        lax.fori_loop(0, F // 2, gather, 0)
        for c in back_copies(i):
            c.start()

    def give_back(i, who):
        return remote(
            fin.at[pl.ds(GIVE * who, GIVE), lanes(i)],
            out_ref.at[0, pl.ds(KEEP, GIVE), lanes(i)],
            gs.at[i, who],
            gr.at[i],
            (who, b),
        )

    def ocean_out(i):
        F = CHUNKS[i]
        for g in range(PAIRS // 8):
            for j in range(F // 2):
                x0 = flux[i][pl.ds(8 * g * F + 2 * j, 8, stride=F), :]
                x1 = flux[i][pl.ds(8 * g * F + 2 * j + 1, 8, stride=F), :]
                at = g * (FIELDS // 2) + starts[i] // 2 + j
                buf = mix.at[at % 8]
                buf[pl.ds(0, 8, stride=2), :] = jnp.where(low, x0, pltpu.roll(x1, CELLS, 1))
                buf[pl.ds(1, 8, stride=2), :] = jnp.where(low, pltpu.roll(x0, CELLS, 1), x1)
                out_ref[0, pl.ds(16 * g, 16), pl.ds(starts[i] * CELLS + 128 * j, 128)] = buf[
                    pl.ds(0, 16), :
                ]

    def finish(i):
        for c in back_copies(i):
            c.wait_recv()

        @pl.when(jnp.logical_not(taker))
        def _():
            out_ref[0, keep_rows, lanes(i)] = tot[i][1] + rec[i][0] + rec[i][1]

        @pl.when(taker)
        def _():
            fin[:, lanes(i)] = tot[i][1] + rec[i][0] + rec[i][1]
            for who in range(SECS - 1):
                give_back(i, who).start()

    for i in range(n):
        forward(i)
        prepare_ocean(i)
        reduce_chip(i)
    for i in range(n):
        fluxes(i)
        backward(i)

    @pl.when(taker)
    def _():
        for i in range(n):
            ocean_out(i)

    for i in range(n):
        finish(i)

    for i in range(n):
        for c in to_neighbours(i, band_in[i].at[1]):
            c.wait_send()
        sib_copy(i).wait_send()
        y_copy(i).wait_send()
        flux_copy(i, core).wait_send()
        for c in back_copies(i):
            c.wait_send()

    @pl.when(taker)
    def _():
        for i in range(n):
            for who in range(SECS - 1):
                ocean_to(i, who).wait_send()
                give_back(i, who).wait_send()

    @pl.when(jnp.logical_not(taker))
    def _():
        for i in range(n):
            hand_over(i, s).wait_send()
            give_back(i, 0).wait_recv()


def on_device(surface, remap_weights, src_tiles, block_count, land_sea, exchange_coef):
    n = len(CHUNKS)
    band, section = lax.axis_index("tile"), lax.axis_index("sec")
    valid = jnp.arange(BLOCKS)[None, :] < block_count[:, None]
    source_sec = src_tiles // (BANDS * TILES)
    within = src_tiles % (BANDS * TILES)
    slot = (within // TILES - band + 1 + BANDS) % BANDS
    row = within % TILES
    kept = row < KEEP
    owner = jnp.where(kept, source_sec, SECS - 1)
    local = jnp.where(kept, row, source_sec * GIVE + row - KEEP)
    index = jnp.where(valid & (owner == section), slot * KEEP + local, SLOTS)
    columns = index.reshape(TILES, BLOCKS // 2, 2).transpose(2, 0, 1).reshape(1, TILES * BLOCKS)
    wet = land_sea.astype(f32).reshape(PAIRS, 2 * CELLS)
    weights = (
        remap_weights.reshape(TILES, BLOCKS, CELLS // 2, 128)
        .transpose(0, 2, 1, 3)
        .reshape(TILES, BLOCKS * CELLS // 2, 128)
    )
    top = max(CHUNKS)
    scratch = [
        pltpu.VMEM((TILES, BLOCKS * CELLS // 2, 128), f32),
        pltpu.VMEM((TILES, BLOCKS * CELLS, 128), bf16),
        pltpu.VMEM((BLOCKS, CELLS, 128), f32),
        pltpu.VMEM((SLOTS, TILES * BLOCKS), bf16),
        pltpu.VMEM((TILES * BLOCKS // 2 * top, 128), f32),
        pltpu.VMEM((HALF, 128), f32),
        pltpu.VMEM((HALF * top, 128), f32),
        pltpu.VMEM((KEEP, WIDE), f32),
    ]
    for F in CHUNKS:
        scratch += [
            pltpu.VMEM((3, KEEP, F * CELLS), f32),
            pltpu.VMEM((PAIRS * F, 128), f32),
            pltpu.VMEM((HALF * F, 128), f32),
            pltpu.VMEM((HALF * F, 128), f32),
            pltpu.VMEM((HALF * F, 128), f32),
            pltpu.VMEM((PAIRS * F, 128), f32),
            pltpu.VMEM((2 * HALF, F * CELLS), f32),
            pltpu.VMEM((2 * HALF * F, 128), f32),
            pltpu.VMEM((3, KEEP, F * CELLS), f32),
            pltpu.VMEM((2, KEEP, F * CELLS), f32),
            pltpu.VMEM((SLOTS + 1, F, 128), f32),
        ]
    sem = pltpu.SemaphoreType.DMA
    scratch += [
        sem((W_PARTS,)),
        sem((n,)),
        sem((n, 2)),
        sem((n, 2)),
        sem((n,)),
        sem((n, SECS - 1)),
        sem((n, SECS - 1)),
        sem((n,)),
        sem((n,)),
        sem((n,)),
        sem((n,)),
        sem((n,)),
        sem((n,)),
        sem((n,)),
        sem((n,)),
        sem((n, 2)),
        sem((n, 2)),
        sem((n, SECS - 1)),
        sem((n,)),
    ]
    vmem = pl.BlockSpec(memory_space=pltpu.VMEM)
    anywhere = pl.BlockSpec(memory_space=pl.ANY)
    smem = pl.BlockSpec(memory_space=pltpu.SMEM)
    return pl.pallas_call(
        kernel,
        out_shape=jax.ShapeDtypeStruct((1, TILES, WIDE), f32),
        in_specs=[anywhere, anywhere, smem, vmem, vmem, vmem],
        out_specs=vmem,
        scratch_shapes=scratch,
        compiler_params=pltpu.CompilerParams(
            collective_id=0, has_side_effects=True, vmem_limit_bytes=56 * 2**20
        ),
    )(surface, weights, index.reshape(-1), columns, wet, exchange_coef[:, None])


def solution(mesh):
    placed = (
        P("sec", "tile", None),
        P("tile", None, None),
        P("tile", None),
        P("tile"),
        P("tile", None),
        P(),
    )
    return jax.shard_map(
        on_device, mesh=mesh, in_specs=placed, out_specs=P("sec", "tile", None), check_vma=False
    )
```

time: 315 us -> 102 us (0.32)
  waiting for transfers between devices: 151 us -> 0 us
  Pallas kernels: 0 us -> 94.4 us
  matrix products: 69.1 us -> 0 us
  local copies, waits for them, and re-layouts: 47.6 us -> 5.52 us
  other arithmetic: 17.7 us -> 1.48 us
  starting transfers between devices: 14.7 us -> 0 us
  between operations: 13.5 us -> 0.02 us
    pallas_call x0 -> x1, Pallas kernels: none -> 94.4 us  [on_device(): pl.pallas_call(kernel, out_shape=jax.ShapeDtypeStruct((1, TILES, WIDE), f...]
    dot_general x2 -> x0, matrix products: 69.1 us -> none  [the longest x1 52.5 us: on_device(): jnp.einsum('tfd,tkcd->tkfc', shared_flux, weights, precision=lax.Precisio...]
    ppermute x4 -> x0, waiting for transfers between devices: 63.1 us -> none  [the longest x1 41.5 us: extended_2(): before = lax.ppermute(last, axis, up)]
    psum x1 -> x0, waiting for transfers between devices: 44.8 us -> none  [spread(): return lax.psum(jnp.where(mine, array, jnp.zeros_like(array)), axis)]
    all_gather x1 -> x0, waiting for transfers between devices: 42.1 us -> none  [on_device(): every = lax.all_gather(surface, 'sec', axis=0, tiled=True)]
    reshape x4, local copies, waits for them, and re-layouts: 25.2 us -> 2.13 us  [the longest x2 0.78 us: on_device(): index.reshape(TILES, BLOCKS // 2, 2).transpose(2, 0, 1)]
    gather x2 -> x0, local copies, waits for them, and re-layouts: 18.2 us -> none  [on_device(): picked = rows[source_sec * 3 * tile_dev + local_row]]
    ppermute x4 -> x0, starting transfers between devices: 14.7 us -> none  [the longest x2 7.39 us: from_behind(): return lax.ppermute(block, axis, route)]
  transfers between devices with their start and end apart: 6 -> 0, of which waited for: 5 -> 0; matrix products, arithmetic and copies ran while one was open for 5% -> 0% of each run, Pallas kernels for 0% -> 0%
where the time goes in v1:
time: 102 us; the launch traced here: 101 us
  Pallas kernels  94.4 us (93%)
  local copies, waits for them, and re-layouts  5.52 us (5%)
  other arithmetic  1.48 us (1%)
    pallas_call x1, Pallas kernels, on_device(): pl.pallas_call(kernel, out_shape=jax.ShapeDtypeStruct((1, TILES, WIDE), f...  94.4 us

profile of v1, /device:TPU:1, one launch (start us, length us, event | category | flops | bytes accessed | tf_op | source)
XLA Modules:
  0.0 101.4 jit_solution(5643777357995991405)
XLA Ops:
  0.0 0.7 fusion.2
  0.7 1.3 %copy.11.coef_ref = f32[40,1]{1,0:T(8,128)} copy(f32[40,1]{0,1:T(1,128)} %bitcast.11) | data formatting | bytes 320 | tf_op jit(solution)/shard_map/broadcast_in_dim | solution.py:482
  2.1 0.1 copy.9
  2.1 0.7 reshape.21.idx_ref
  2.8 0.8 convert_element_type.3
  3.6 0.7 reshape.24.wet_ref
  4.3 0.1 copy.10
  4.4 0.7 reshape.23.col_ref
  5.0 94.4 %shard_map.64 = f32[1,64,2560]{2,1,0:T(8,128)} custom-call(f32[1,64,2560]{2,1,0:T(8,128)} %x_ref.1, f32[64,256,128]{2,1,0:T(8,128)} %bitcast.8, s32[512]{0:T(512)} %reshape.21.idx_ref, s32[1,512]{1,0:T(1,128)} %reshape.23.col_ref, f32[32,128]{1,0:T(8,128)} %reshape.24.wet_ref, f32[40,1]{1,0:T(8,128)} %copy.11.coef_ref), custom_call_target="tpu_custom_call" | custom-call | tf_op jit(solution)/shard_map/pallas_call | solution.py:473
  99.4 2.0 %copy.13 = f32[1,64,2560]{2,1,0:T(8,128)} copy(f32[1,64,2560]{2,1,0:T(8,128)} %shard_map.64) | data formatting | bytes 1310720

commit v2 on v1

--- a/solution.py
+++ b/solution.py
@@ -17,6 +17,7 @@
 HALF = PAIRS // 2
 CHUNKS = (16, 24)
 W_PARTS = 8
+RING = 4
 f32, bf16 = jnp.float32, jnp.bfloat16
 
 
@@ -25,12 +26,13 @@
     return hi, x - hi
 
 
-def kernel(x_ref, w_ref, idx_ref, col_ref, wet_ref, coef_ref, out_ref, *scratch):
+def kernel(x_ref, w_ref, ids_ref, used_ref, land_ref, coef_ref, out_ref, *scratch):
     n = len(CHUNKS)
     (wraw, wp, mix, hot, cb, fac, rel, fin) = scratch[:8]
-    per = scratch[8 : 8 + 11 * n]
-    (w_sem, own_sem, xs, xr, hs, hr, oss, orr, osl, s1s, s1r, ys, yr, s2s, s2r, bs, br, gs, gr) = (
-        scratch[8 + 11 * n :]
+    (ids, used, land, coef_in, index, idx, wet, coef) = scratch[8:16]
+    per = scratch[16 : 16 + 11 * n]
+    (small, w_sem, own_sem, xs, xr, hs, hr, oss, orr, osl, s1s, s1r, ys, yr, s2s, s2r, bs, br, gs, gr) = (
+        scratch[16 + 11 * n :]
     )
     band_in, part, sib, ysum, yrec, flux, oc, ocd, tot, rec, src = [
         [per[11 * i + j] for i in range(n)] for j in range(11)
@@ -41,6 +43,9 @@
     opp = lax.rem(s + 2, SECS)
     east, west = lax.rem(b + 1, BANDS), lax.rem(b + BANDS - 1, BANDS)
     taker = s == SECS - 1
+    x = lax.rem(b, RING)
+    east_sec = jnp.where(x == RING - 1, opp, s)
+    west_sec = jnp.where(x == 0, opp, s)
     lane = lax.broadcasted_iota(jnp.int32, (1, 128), 1)
     low = lane < CELLS
     starts = [sum(CHUNKS[:i]) for i in range(n)]
@@ -68,8 +73,8 @@
 
     def to_neighbours(i, block):
         return (
-            remote(block, band_in[i].at[0], xs.at[i, 0], xr.at[i, 0], (s, east)),
-            remote(block, band_in[i].at[2], xs.at[i, 1], xr.at[i, 1], (s, west)),
+            remote(block, band_in[i].at[0], xs.at[i, 0], xr.at[i, 0], (east_sec, east)),
+            remote(block, band_in[i].at[2], xs.at[i, 1], xr.at[i, 1], (west_sec, west)),
         )
 
     def hand_over(i, who):
@@ -81,20 +86,31 @@
             (SECS - 1, b),
         )
 
-    def ocean_to(i, who):
+    def ocean_to(i, who, z):
         return remote(
-            x_ref.at[0, pl.ds((who % 2) * 2 * HALF, 2 * HALF), lanes(i)],
-            oc[i],
-            oss.at[i, who],
-            orr.at[i],
+            x_ref.at[0, pl.ds((who % 2) * HALF + z * PAIRS, HALF), lanes(i)],
+            oc[i].at[pl.ds(z * HALF, HALF)],
+            oss.at[i, who, z],
+            orr.at[i, z],
             (who, b),
         )
 
-    def ocean_own(i):
+    def ocean_own(i, z):
         return pltpu.make_async_copy(
-            x_ref.at[0, pl.ds(2 * HALF, 2 * HALF), lanes(i)], oc[i], osl.at[i]
-        )
-
+            x_ref.at[0, pl.ds(HALF + z * PAIRS, HALF), lanes(i)],
+            oc[i].at[pl.ds(z * HALF, HALF)],
+            osl.at[i, z],
+        )
+
+    tables = [
+        pltpu.make_async_copy(a, z, small.at[j])
+        for j, (a, z) in enumerate(
+            ((ids_ref, ids), (used_ref, used), (land_ref, land), (coef_ref, coef_in))
+        )
+    ]
+
+    for c in tables:
+        c.start()
     for c in w_copy:
         c.start()
 
@@ -106,21 +122,23 @@
     @pl.when(taker)
     def _():
         for i in range(n):
-            ocean_own(i).start()
+            for z in range(2):
+                ocean_own(i, z).start()
 
     barrier = pltpu.get_barrier_semaphore()
     for q in (1, 2, 3):
         pl.semaphore_signal(
             barrier, inc=1, device_id=(lax.rem(s + q, SECS), b), device_id_type=MESH
         )
-    for z in (east, west):
-        pl.semaphore_signal(barrier, inc=1, device_id=(s, z), device_id_type=MESH)
+    for z in ((east_sec, east), (west_sec, west)):
+        pl.semaphore_signal(barrier, inc=1, device_id=z, device_id_type=MESH)
     pl.semaphore_wait(barrier, 5)
 
     @pl.when(jnp.logical_not(taker))
     def _():
         for i in range(n):
             hand_over(i, s).start()
+        for i in range(n):
             for c in to_neighbours(i, x_ref.at[0, keep_rows, lanes(i)]):
                 c.start()
 
@@ -145,7 +163,7 @@
 
     def prepare_part(i):
         w_copy[i].wait()
-        lax.fori_loop(i * per_w, (i + 1) * per_w, prepare, 0)
+        lax.fori_loop(i * per_w, (i + 1) * per_w, prepare, 0, unroll=4)
 
     take_over(0)
 
@@ -153,15 +171,43 @@
     def _():
         for i in range(n):
             for who in range(SECS - 1):
-                ocean_to(i, who).start()
+                for z in range(2):
+                    ocean_to(i, who, z).start()
+
+    for c in tables:
+        c.wait()
+    sec_tiles = BANDS * TILES
+    source = ids[...] // sec_tiles
+    within = ids[...] % sec_tiles
+    slot = (within // TILES - b + 1 + BANDS) % BANDS
+    row = within % TILES
+    kept = row < KEEP
+    owner = jnp.where(kept, source, SECS - 1)
+    local = jnp.where(kept, row, source * GIVE + row - KEEP)
+    holder = jnp.where(slot == 0, west_sec, jnp.where(slot == 2, east_sec, s))
+    valid = lax.broadcasted_iota(jnp.int32, (BLOCKS, TILES), 0) < used[...]
+    named = jnp.where(valid & (owner == holder), slot * KEEP + local, SLOTS)
+    index[...] = jnp.concatenate([named, named], axis=1)
+    to_smem = pltpu.make_async_copy(index, idx, small.at[len(tables)])
+    to_smem.start()
+    rows = lax.broadcasted_iota(jnp.int32, (SLOTS, 128), 0)
+    for kpar in range(2):
+        for h in range(2):
+            k = 4 * h + kpar
+            named = jnp.where(low, index[pl.ds(k, 1), :], index[pl.ds(k + 2, 1), :])
+            at = pl.ds(128 * (2 * kpar + h), 128)
+            hot[:, at] = jnp.where(rows == named, 1.0, 0.0).astype(bf16)
+    dry = land[...].astype(f32)
+    wet[...] = jnp.concatenate([dry[:PAIRS], dry[PAIRS:]], axis=1)
+    square = [lax.broadcasted_iota(jnp.int32, (FIELDS, FIELDS), d) for d in range(2)]
+    diagonal = jnp.where(square[0] == square[1], coef_in[...], 0.0)
+    coef[...] = jnp.broadcast_to(jnp.sum(diagonal, axis=1, keepdims=True), (FIELDS, 128))
 
     for i in range(W_PARTS):
         prepare_part(i)
         if i + 1 < n:
             take_over(i + 1)
-
-    rows = lax.broadcasted_iota(jnp.int32, (SLOTS, TILES * BLOCKS), 0)
-    hot[...] = jnp.where(rows == col_ref[...], 1.0, 0.0).astype(bf16)
+    to_smem.wait()
 
     def spread(view, count, F, dst, base):
         for g in range(count // 8):
@@ -191,11 +237,11 @@
         def pair(p, _):
             q = []
             for tp in range(2):
-                t = 2 * p + tp
+                t = p + PAIRS * tp
                 cols = []
                 for kp in range(BLOCKS // 2):
-                    g0 = idx_ref[t * BLOCKS + 2 * kp]
-                    g1 = idx_ref[t * BLOCKS + 2 * kp + 1]
+                    g0 = idx[2 * kp, t]
+                    g1 = idx[2 * kp + 1, t]
                     cols.append(
                         jnp.where(
                             low,
@@ -213,9 +259,9 @@
             return 0
 
         first = (1 - core) * HALF
-        lax.fori_loop(0, HALF, lambda u, c: pair(first + u, c), 0)
+        lax.fori_loop(0, HALF, lambda u, c: pair(first + u, c), 0, unroll=8)
         sib_copy(i).start()
-        lax.fori_loop(0, HALF, lambda u, c: pair(core * HALF + u, c), 0)
+        lax.fori_loop(0, HALF, lambda u, c: pair(core * HALF + u, c), 0, unroll=8)
 
     def half_rows(i, which):
         size = HALF * CHUNKS[i]
@@ -241,11 +287,13 @@
     def prepare_ocean(i):
         @pl.when(taker)
         def _():
-            ocean_own(i).wait()
+            for z in range(2):
+                ocean_own(i, z).wait()
 
         @pl.when(jnp.logical_not(taker))
         def _():
-            ocean_to(i, 0).wait_recv()
+            for z in range(2):
+                ocean_to(i, 0, z).wait_recv()
 
         spread(oc[i], 2 * HALF, CHUNKS[i], ocd[i], 0)
 
@@ -255,8 +303,8 @@
 
         def relative(u, _):
             at = pl.ds(pl.multiple_of(u * F, 8), F)
-            a = ocd[i][pl.ds(pl.multiple_of(2 * u * F, 8), F), :]
-            z = ocd[i][pl.ds(pl.multiple_of((2 * u + 1) * F, 8), F), :]
+            a = ocd[i][pl.ds(pl.multiple_of(u * F, 8), F), :]
+            z = ocd[i][pl.ds(pl.multiple_of((HALF + u) * F, 8), F), :]
             rel[at, :] = ysum[i][at, :] + yrec[i][at, :] - jnp.where(low, a, z)
             return 0
 
@@ -265,14 +313,13 @@
             r0, r1, r2 = [rel[pl.ds(f, HALF, stride=F), :] for f in range(3)]
             speed = jnp.sqrt(r0 * r0 + r1 * r1 + 0.25)
             stab = 1.0 + 0.5 * jnp.tanh(-r2)
-            wet = wet_ref[pl.ds(pl.multiple_of(core * HALF, 8), HALF), :]
-            fac[...] = speed * stab * wet
-        coef = jnp.broadcast_to(coef_ref[pl.ds(starts[i], F), :], (F, 128))
+            fac[...] = speed * stab * wet[pl.ds(pl.multiple_of(core * HALF, 8), HALF), :]
+        exchange = coef[pl.ds(starts[i], F), :]
 
         def scale(u, _):
             at = pl.ds(pl.multiple_of(u * F, 8), F)
             to = pl.ds(pl.multiple_of((core * HALF + u) * F, 8), F)
-            flux[i][to, :] = coef * fac[pl.ds(u, 1), :] * rel[at, :]
+            flux[i][to, :] = exchange * fac[pl.ds(u, 1), :] * rel[at, :]
             return 0
 
         lax.fori_loop(0, HALF, scale, 0)
@@ -280,8 +327,8 @@
 
     def back_copies(i):
         return (
-            remote(tot[i].at[0], rec[i].at[1], bs.at[i, 0], br.at[i, 1], (s, west)),
-            remote(tot[i].at[2], rec[i].at[0], bs.at[i, 1], br.at[i, 0], (s, east)),
+            remote(tot[i].at[0], rec[i].at[1], bs.at[i, 0], br.at[i, 1], (west_sec, west)),
+            remote(tot[i].at[2], rec[i].at[0], bs.at[i, 1], br.at[i, 0], (east_sec, east)),
         )
 
     def backward(i):
@@ -292,7 +339,7 @@
             v = flux[i][pl.ds(pl.multiple_of(p * F, 8), F), :]
             r = pltpu.roll(v, CELLS, 1)
             for tp in range(2):
-                t = 2 * p + tp
+                t = p + PAIRS * tp
                 hi, lo = split(jnp.where(low, v, r) if tp == 0 else jnp.where(low, r, v))
                 lhs = jnp.concatenate([hi, lo], axis=0).astype(bf16)
                 o = lax.dot_general(
@@ -300,11 +347,11 @@
                 )
                 o = o[:F] + o[F:]
                 for kp in range(BLOCKS // 2):
-                    at = pl.multiple_of((t * (BLOCKS // 2) + kp) * F, 8)
+                    at = pl.multiple_of((kp * TILES + t) * F, 8)
                     cb[pl.ds(at, F), :] = o[:, 128 * kp : 128 * kp + 128]
             return 0
 
-        lax.fori_loop(0, PAIRS, pair, 0)
+        lax.fori_loop(0, PAIRS, pair, 0, unroll=8)
 
         def gather(j, _):
             count = TILES * BLOCKS // 2
@@ -321,7 +368,7 @@
                 tot[i][z, :, at] = o[z * KEEP : (z + 1) * KEEP]
             return 0
 
-        lax.fori_loop(0, F // 2, gather, 0)
+        lax.fori_loop(0, F // 2, gather, 0, unroll=4)
         for c in back_copies(i):
             c.start()
 
@@ -340,13 +387,11 @@
             for j in range(F // 2):
                 x0 = flux[i][pl.ds(8 * g * F + 2 * j, 8, stride=F), :]
                 x1 = flux[i][pl.ds(8 * g * F + 2 * j + 1, 8, stride=F), :]
-                at = g * (FIELDS // 2) + starts[i] // 2 + j
-                buf = mix.at[at % 8]
-                buf[pl.ds(0, 8, stride=2), :] = jnp.where(low, x0, pltpu.roll(x1, CELLS, 1))
-                buf[pl.ds(1, 8, stride=2), :] = jnp.where(low, pltpu.roll(x0, CELLS, 1), x1)
-                out_ref[0, pl.ds(16 * g, 16), pl.ds(starts[i] * CELLS + 128 * j, 128)] = buf[
-                    pl.ds(0, 16), :
-                ]
+                at = pl.ds(starts[i] * CELLS + 128 * j, 128)
+                out_ref[0, pl.ds(8 * g, 8), at] = jnp.where(low, x0, pltpu.roll(x1, CELLS, 1))
+                out_ref[0, pl.ds(PAIRS + 8 * g, 8), at] = jnp.where(
+                    low, pltpu.roll(x0, CELLS, 1), x1
+                )
 
     def finish(i):
         for c in back_copies(i):
@@ -391,7 +436,8 @@
     def _():
         for i in range(n):
             for who in range(SECS - 1):
-                ocean_to(i, who).wait_send()
+                for z in range(2):
+                    ocean_to(i, who, z).wait_send()
                 give_back(i, who).wait_send()
 
     @pl.when(jnp.logical_not(taker))
@@ -403,18 +449,6 @@
 
 def on_device(surface, remap_weights, src_tiles, block_count, land_sea, exchange_coef):
     n = len(CHUNKS)
-    band, section = lax.axis_index("tile"), lax.axis_index("sec")
-    valid = jnp.arange(BLOCKS)[None, :] < block_count[:, None]
-    source_sec = src_tiles // (BANDS * TILES)
-    within = src_tiles % (BANDS * TILES)
-    slot = (within // TILES - band + 1 + BANDS) % BANDS
-    row = within % TILES
-    kept = row < KEEP
-    owner = jnp.where(kept, source_sec, SECS - 1)
-    local = jnp.where(kept, row, source_sec * GIVE + row - KEEP)
-    index = jnp.where(valid & (owner == section), slot * KEEP + local, SLOTS)
-    columns = index.reshape(TILES, BLOCKS // 2, 2).transpose(2, 0, 1).reshape(1, TILES * BLOCKS)
-    wet = land_sea.astype(f32).reshape(PAIRS, 2 * CELLS)
     weights = (
         remap_weights.reshape(TILES, BLOCKS, CELLS // 2, 128)
         .transpose(0, 2, 1, 3)
@@ -430,6 +464,14 @@
         pltpu.VMEM((HALF, 128), f32),
         pltpu.VMEM((HALF * top, 128), f32),
         pltpu.VMEM((KEEP, WIDE), f32),
+        pltpu.VMEM((BLOCKS, TILES), jnp.int32),
+        pltpu.VMEM((1, TILES), jnp.int32),
+        pltpu.VMEM((TILES, CELLS), jnp.int32),
+        pltpu.VMEM((1, FIELDS), f32),
+        pltpu.VMEM((BLOCKS, 128), jnp.int32),
+        pltpu.SMEM((BLOCKS, 128), jnp.int32),
+        pltpu.VMEM((PAIRS, 128), f32),
+        pltpu.VMEM((FIELDS, 128), f32),
     ]
     for F in CHUNKS:
         scratch += [
@@ -446,40 +488,32 @@
             pltpu.VMEM((SLOTS + 1, F, 128), f32),
         ]
     sem = pltpu.SemaphoreType.DMA
-    scratch += [
-        sem((W_PARTS,)),
-        sem((n,)),
-        sem((n, 2)),
-        sem((n, 2)),
-        sem((n,)),
-        sem((n, SECS - 1)),
-        sem((n, SECS - 1)),
-        sem((n,)),
-        sem((n,)),
-        sem((n,)),
-        sem((n,)),
-        sem((n,)),
-        sem((n,)),
-        sem((n,)),
-        sem((n,)),
-        sem((n, 2)),
-        sem((n, 2)),
-        sem((n, SECS - 1)),
-        sem((n,)),
-    ]
+    shapes = {
+        "small": (5,), "w": (W_PARTS,), "own": (n,), "xs": (n, 2), "xr": (n, 2),
+        "hs": (n,), "hr": (n, SECS - 1), "oss": (n, SECS - 1, 2), "orr": (n, 2), "osl": (n, 2),
+        "s1s": (n,), "s1r": (n,), "ys": (n,), "yr": (n,), "s2s": (n,), "s2r": (n,),
+        "bs": (n, 2), "br": (n, 2), "gs": (n, SECS - 1), "gr": (n,),
+    }
+    scratch += [sem(shape) for shape in shapes.values()]
     vmem = pl.BlockSpec(memory_space=pltpu.VMEM)
     anywhere = pl.BlockSpec(memory_space=pl.ANY)
-    smem = pl.BlockSpec(memory_space=pltpu.SMEM)
     return pl.pallas_call(
         kernel,
         out_shape=jax.ShapeDtypeStruct((1, TILES, WIDE), f32),
-        in_specs=[anywhere, anywhere, smem, vmem, vmem, vmem],
+        in_specs=[anywhere] * 6,
         out_specs=vmem,
         scratch_shapes=scratch,
         compiler_params=pltpu.CompilerParams(
             collective_id=0, has_side_effects=True, vmem_limit_bytes=56 * 2**20
         ),
-    )(surface, weights, index.reshape(-1), columns, wet, exchange_coef[:, None])
+    )(
+        surface,
+        weights,
+        src_tiles.T,
+        block_count[None],
+        land_sea,
+        exchange_coef[None],
+    )
 
 
 def solution(mesh):

time: 102 us -> 59.5 us (0.58)
  Pallas kernels: 94.4 us -> 57.5 us
  local copies, waits for them, and re-layouts: 5.52 us -> 1.97 us
  other arithmetic: 1.48 us -> 0 us
    pallas_call x1, Pallas kernels: 94.4 us -> 57.5 us  [on_device(): pl.pallas_call(kernel, out_shape=jax.ShapeDtypeStruct((1, TILES, WIDE), f...]
    reshape x4 -> x0, local copies, waits for them, and re-layouts: 2.13 us -> none  [the longest x2 0.78 us: on_device(): index.reshape(TILES, BLOCKS // 2, 2).transpose(2, 0, 1)]
    broadcast_in_dim x1 -> x0, local copies, waits for them, and re-layouts: 1.34 us -> none  [on_device(): exchange_coef[:, None]]
where the time goes in v2:
time: 59.5 us; the launch traced here: 59.4 us
  Pallas kernels  57.5 us (97%)
  local copies, waits for them, and re-layouts  1.97 us (3%)
    pallas_call x1, Pallas kernels, on_device(): pl.pallas_call(kernel, out_shape=jax.ShapeDtypeStruct((1, TILES, WIDE), f...  57.5 us
    unnamed x1, local copies, waits for them, and re-layouts  1.97 us

profile of v2, /device:TPU:1, one launch (start us, length us, event | category | flops | bytes accessed | tf_op | source)
XLA Modules:
  0.0 59.4 jit_solution(18295854788406875863)
XLA Ops:
  0.0 57.5 %shard_map.64 = f32[1,64,2560]{2,1,0:T(8,128)} custom-call(f32[1,64,2560]{2,1,0:T(8,128)} %x_ref.1, f32[64,256,128]{2,1,0:T(8,128)} %bitcast.8, s32[8,64]{1,0:T(8,128)} %bitcast.9, s32[1,64]{1,0:T(1,128)} %bitcast.10, s32[64,64]{1,0:T(8,128)} %land_ref.1, f32[1,40]{1,0:T(1,128)} %bitcast.11), custom_call_target="tpu_custom_call" | custom-call | tf_op jit(solution)/shard_map/pallas_call | solution.py:500
  57.5 2.0 %copy.8 = f32[1,64,2560]{2,1,0:T(8,128)} copy(f32[1,64,2560]{2,1,0:T(8,128)} %shard_map.64) | data formatting | bytes 1310720

commit v3 on v2

--- a/solution.py
+++ b/solution.py
@@ -15,6 +15,8 @@
 SLOTS = 3 * KEEP
 PAIRS = TILES // 2
 HALF = PAIRS // 2
+STEPS = 2
+STEP = HALF // STEPS
 CHUNKS = (16, 24)
 W_PARTS = 8
 RING = 4
@@ -28,14 +30,14 @@
 
 def kernel(x_ref, w_ref, ids_ref, used_ref, land_ref, coef_ref, out_ref, *scratch):
     n = len(CHUNKS)
-    (wraw, wp, mix, hot, cb, fac, rel, fin) = scratch[:8]
-    (ids, used, land, coef_in, index, idx, wet, coef) = scratch[8:16]
-    per = scratch[16 : 16 + 11 * n]
+    (wraw, wp, mix, hot, cb, fac, rel) = scratch[:7]
+    (ids, used, land, coef_in, index, idx, wet, coef) = scratch[7:15]
+    per = scratch[15 : 15 + 12 * n]
     (small, w_sem, own_sem, xs, xr, hs, hr, oss, orr, osl, s1s, s1r, ys, yr, s2s, s2r, bs, br, gs, gr) = (
-        scratch[16 + 11 * n :]
+        scratch[15 + 12 * n :]
     )
-    band_in, part, sib, ysum, yrec, flux, oc, ocd, tot, rec, src = [
-        [per[11 * i + j] for i in range(n)] for j in range(11)
+    band_in, part, sib, ysum, yrec, flux, oc, ocd, tot, rec, src, given = [
+        [per[12 * i + j] for i in range(n)] for j in range(12)
     ]
     s, b = lax.axis_index("sec"), lax.axis_index("tile")
     core = lax.rem(s, 2)
@@ -109,6 +111,16 @@
         )
     ]
 
+    barrier = pltpu.get_barrier_semaphore()
+    for q in (1, 2, 3):
+        pl.semaphore_signal(
+            barrier, inc=1, device_id=(lax.rem(s + q, SECS), b), device_id_type=MESH
+        )
+    for z in (east, west):
+        for q in range(SECS):
+            pl.semaphore_signal(
+                barrier, inc=1, device_id=(lax.rem(s + q, SECS), z), device_id_type=MESH
+            )
     for c in tables:
         c.start()
     for c in w_copy:
@@ -125,14 +137,7 @@
             for z in range(2):
                 ocean_own(i, z).start()
 
-    barrier = pltpu.get_barrier_semaphore()
-    for q in (1, 2, 3):
-        pl.semaphore_signal(
-            barrier, inc=1, device_id=(lax.rem(s + q, SECS), b), device_id_type=MESH
-        )
-    for z in ((east_sec, east), (west_sec, west)):
-        pl.semaphore_signal(barrier, inc=1, device_id=z, device_id_type=MESH)
-    pl.semaphore_wait(barrier, 5)
+    pl.semaphore_wait(barrier, 3 * SECS - 1)
 
     @pl.when(jnp.logical_not(taker))
     def _():
@@ -258,31 +263,50 @@
             )
             return 0
 
-        first = (1 - core) * HALF
-        lax.fori_loop(0, HALF, lambda u, c: pair(first + u, c), 0, unroll=8)
-        sib_copy(i).start()
-        lax.fori_loop(0, HALF, lambda u, c: pair(core * HALF + u, c), 0, unroll=8)
-
-    def half_rows(i, which):
-        size = HALF * CHUNKS[i]
-        return pl.ds(pl.multiple_of(which * size, 8), size)
-
-    def sib_copy(i):
+        def other(q, _):
+            lax.fori_loop(
+                0, STEP, lambda u, c: pair((1 - core) * HALF + q * STEP + u, c), 0, unroll=STEP
+            )
+            sib_copy(i, q).start()
+            return 0
+
+        def own(q, _):
+            lax.fori_loop(
+                0, STEP, lambda u, c: pair(core * HALF + q * STEP + u, c), 0, unroll=STEP
+            )
+            at = step_rows(i, q)
+            sib_copy(i, q).wait_recv()
+            ysum[i][at, :] = part[i][half_rows(i, core, q), :] + sib[i][at, :]
+            y_copy(i, q).start()
+            return 0
+
+        lax.fori_loop(0, STEPS, other, 0)
+        lax.fori_loop(0, STEPS, own, 0)
+
+    def step_rows(i, q):
+        size = STEP * CHUNKS[i]
+        return pl.ds(pl.multiple_of(q * size, 8), size)
+
+    def half_rows(i, which, q):
+        size = STEP * CHUNKS[i]
+        return pl.ds(pl.multiple_of((which * STEPS + q) * size, 8), size)
+
+    def sib_copy(i, q):
         return remote(
-            part[i].at[half_rows(i, 1 - core)], sib[i], s1s.at[i], s1r.at[i], (mate, b)
-        )
-
-    def y_copy(i):
-        return remote(ysum[i], yrec[i], ys.at[i], yr.at[i], (opp, b))
-
-    def flux_copy(i, which):
-        at = flux[i].at[half_rows(i, which)]
-        return remote(at, at, s2s.at[i], s2r.at[i], (mate, b))
-
-    def reduce_chip(i):
-        sib_copy(i).wait_recv()
-        ysum[i][...] = part[i][half_rows(i, core), :] + sib[i][...]
-        y_copy(i).start()
+            part[i].at[half_rows(i, 1 - core, q)],
+            sib[i].at[step_rows(i, q)],
+            s1s.at[i, q],
+            s1r.at[i, q],
+            (mate, b),
+        )
+
+    def y_copy(i, q):
+        at = step_rows(i, q)
+        return remote(ysum[i].at[at], yrec[i].at[at], ys.at[i, q], yr.at[i, q], (opp, b))
+
+    def flux_copy(i, which, q):
+        at = flux[i].at[half_rows(i, which, q)]
+        return remote(at, at, s2s.at[i, q], s2r.at[i, q], (mate, b))
 
     def prepare_ocean(i):
         @pl.when(taker)
@@ -297,43 +321,32 @@
 
         spread(oc[i], 2 * HALF, CHUNKS[i], ocd[i], 0)
 
-    def fluxes(i):
+    def fluxes(i, q):
         F = CHUNKS[i]
-        y_copy(i).wait_recv()
-
-        def relative(u, _):
+        y_copy(i, q).wait_recv()
+        for v in range(STEP):
+            u = q * STEP + v
             at = pl.ds(pl.multiple_of(u * F, 8), F)
-            a = ocd[i][pl.ds(pl.multiple_of(u * F, 8), F), :]
+            a = ocd[i][at, :]
             z = ocd[i][pl.ds(pl.multiple_of((HALF + u) * F, 8), F), :]
             rel[at, :] = ysum[i][at, :] + yrec[i][at, :] - jnp.where(low, a, z)
-            return 0
-
-        lax.fori_loop(0, HALF, relative, 0)
+        here = pl.ds(pl.multiple_of(q * STEP, 8), STEP)
         if i == 0:
-            r0, r1, r2 = [rel[pl.ds(f, HALF, stride=F), :] for f in range(3)]
+            r0, r1, r2 = [rel[pl.ds(q * STEP * F + f, STEP, stride=F), :] for f in range(3)]
             speed = jnp.sqrt(r0 * r0 + r1 * r1 + 0.25)
             stab = 1.0 + 0.5 * jnp.tanh(-r2)
-            fac[...] = speed * stab * wet[pl.ds(pl.multiple_of(core * HALF, 8), HALF), :]
+            sea = wet[pl.ds(pl.multiple_of(core * HALF + q * STEP, 8), STEP), :]
+            fac[here, :] = speed * stab * sea
         exchange = coef[pl.ds(starts[i], F), :]
-
-        def scale(u, _):
+        for v in range(STEP):
+            u = q * STEP + v
             at = pl.ds(pl.multiple_of(u * F, 8), F)
             to = pl.ds(pl.multiple_of((core * HALF + u) * F, 8), F)
             flux[i][to, :] = exchange * fac[pl.ds(u, 1), :] * rel[at, :]
-            return 0
-
-        lax.fori_loop(0, HALF, scale, 0)
-        flux_copy(i, core).start()
-
-    def back_copies(i):
-        return (
-            remote(tot[i].at[0], rec[i].at[1], bs.at[i, 0], br.at[i, 1], (west_sec, west)),
-            remote(tot[i].at[2], rec[i].at[0], bs.at[i, 1], br.at[i, 0], (east_sec, east)),
-        )
+        flux_copy(i, core, q).start()
 
     def backward(i):
         F = CHUNKS[i]
-        flux_copy(i, 1 - core).wait_recv()
 
         def pair(p, _):
             v = flux[i][pl.ds(pl.multiple_of(p * F, 8), F), :]
@@ -351,7 +364,22 @@
                     cb[pl.ds(at, F), :] = o[:, 128 * kp : 128 * kp + 128]
             return 0
 
-        lax.fori_loop(0, PAIRS, pair, 0, unroll=8)
+        def own(q, _):
+            fluxes(i, q)
+            lax.fori_loop(
+                0, STEP, lambda u, c: pair(core * HALF + q * STEP + u, c), 0, unroll=STEP
+            )
+            return 0
+
+        def other(q, _):
+            flux_copy(i, 1 - core, q).wait_recv()
+            lax.fori_loop(
+                0, STEP, lambda u, c: pair((1 - core) * HALF + q * STEP + u, c), 0, unroll=STEP
+            )
+            return 0
+
+        lax.fori_loop(0, STEPS, own, 0)
+        lax.fori_loop(0, STEPS, other, 0)
 
         def gather(j, _):
             count = TILES * BLOCKS // 2
@@ -368,18 +396,48 @@
                 tot[i][z, :, at] = o[z * KEEP : (z + 1) * KEEP]
             return 0
 
-        lax.fori_loop(0, F // 2, gather, 0, unroll=4)
-        for c in back_copies(i):
-            c.start()
-
-    def give_back(i, who):
-        return remote(
-            fin.at[pl.ds(GIVE * who, GIVE), lanes(i)],
-            out_ref.at[0, pl.ds(KEEP, GIVE), lanes(i)],
-            gs.at[i, who],
-            gr.at[i],
-            (who, b),
-        )
+        for g in range(2):
+            lax.fori_loop(g * F // 4, (g + 1) * F // 4, gather, 0, unroll=F // 4)
+            for when, c in back_copies(i, g):
+                pl.when(when)(c.start)
+
+    def back_copies(i, g):
+        size = CHUNKS[i] * CELLS // 2
+        at = pl.ds(g * size, size)
+        copies = []
+        for o, sec, to in ((0, west_sec, west), (2, east_sec, east), (1, s, b)):
+            if o != 1:
+                z = (2 - o) // 2
+                c = remote(
+                    tot[i].at[o, :, at],
+                    rec[i].at[z, :, at],
+                    bs.at[i, g, o],
+                    br.at[i, g, z],
+                    (sec, to),
+                )
+                copies.append((sec != SECS - 1, c))
+            for who in range(SECS - 1):
+                c = remote(
+                    tot[i].at[o, pl.ds(GIVE * who, GIVE), at],
+                    given[i].at[2 - o, :, at],
+                    gs.at[i, g, o, who],
+                    gr.at[i, g, 2 - o],
+                    (who, to),
+                )
+                copies.append((sec == SECS - 1, c))
+        return copies
+
+    def back_arrivals(i, g):
+        size = CHUNKS[i] * CELLS // 2
+        at = pl.ds(g * size, size)
+        copies = []
+        for z in range(2):
+            block = rec[i].at[z, :, at]
+            copies.append(remote(block, block, bs.at[i, g, 0], br.at[i, g, z], (opp, b)))
+        for z in range(3):
+            block = given[i].at[z, :, at]
+            copies.append(remote(block, block, bs.at[i, g, 0], gr.at[i, g, z], (opp, b)))
+        return copies
 
     def ocean_out(i):
         F = CHUNKS[i]
@@ -394,25 +452,16 @@
                 )
 
     def finish(i):
-        for c in back_copies(i):
-            c.wait_recv()
-
-        @pl.when(jnp.logical_not(taker))
-        def _():
-            out_ref[0, keep_rows, lanes(i)] = tot[i][1] + rec[i][0] + rec[i][1]
-
-        @pl.when(taker)
-        def _():
-            fin[:, lanes(i)] = tot[i][1] + rec[i][0] + rec[i][1]
-            for who in range(SECS - 1):
-                give_back(i, who).start()
+        for g in range(2):
+            for c in back_arrivals(i, g):
+                c.wait_recv()
+        out_ref[0, keep_rows, lanes(i)] = tot[i][1] + rec[i][0] + rec[i][1]
+        out_ref[0, give_rows, lanes(i)] = given[i][0] + given[i][1] + given[i][2]
 
     for i in range(n):
         forward(i)
         prepare_ocean(i)
-        reduce_chip(i)
     for i in range(n):
-        fluxes(i)
         backward(i)
 
     @pl.when(taker)
@@ -420,17 +469,21 @@
         for i in range(n):
             ocean_out(i)
 
-    for i in range(n):
-        finish(i)
+    @pl.when(jnp.logical_not(taker))
+    def _():
+        for i in range(n):
+            finish(i)
 
     for i in range(n):
         for c in to_neighbours(i, band_in[i].at[1]):
             c.wait_send()
-        sib_copy(i).wait_send()
-        y_copy(i).wait_send()
-        flux_copy(i, core).wait_send()
-        for c in back_copies(i):
-            c.wait_send()
+        for q in range(STEPS):
+            sib_copy(i, q).wait_send()
+            y_copy(i, q).wait_send()
+            flux_copy(i, core, q).wait_send()
+        for g in range(2):
+            for when, c in back_copies(i, g):
+                pl.when(when)(c.wait_send)
 
     @pl.when(taker)
     def _():
@@ -438,13 +491,11 @@
             for who in range(SECS - 1):
                 for z in range(2):
                     ocean_to(i, who, z).wait_send()
-                give_back(i, who).wait_send()
 
     @pl.when(jnp.logical_not(taker))
     def _():
         for i in range(n):
             hand_over(i, s).wait_send()
-            give_back(i, 0).wait_recv()
 
 
 def on_device(surface, remap_weights, src_tiles, block_count, land_sea, exchange_coef):
@@ -463,7 +514,6 @@
         pltpu.VMEM((TILES * BLOCKS // 2 * top, 128), f32),
         pltpu.VMEM((HALF, 128), f32),
         pltpu.VMEM((HALF * top, 128), f32),
-        pltpu.VMEM((KEEP, WIDE), f32),
         pltpu.VMEM((BLOCKS, TILES), jnp.int32),
         pltpu.VMEM((1, TILES), jnp.int32),
         pltpu.VMEM((TILES, CELLS), jnp.int32),
@@ -486,13 +536,15 @@
             pltpu.VMEM((3, KEEP, F * CELLS), f32),
             pltpu.VMEM((2, KEEP, F * CELLS), f32),
             pltpu.VMEM((SLOTS + 1, F, 128), f32),
+            pltpu.VMEM((3, GIVE, F * CELLS), f32),
         ]
     sem = pltpu.SemaphoreType.DMA
     shapes = {
         "small": (5,), "w": (W_PARTS,), "own": (n,), "xs": (n, 2), "xr": (n, 2),
         "hs": (n,), "hr": (n, SECS - 1), "oss": (n, SECS - 1, 2), "orr": (n, 2), "osl": (n, 2),
-        "s1s": (n,), "s1r": (n,), "ys": (n,), "yr": (n,), "s2s": (n,), "s2r": (n,),
-        "bs": (n, 2), "br": (n, 2), "gs": (n, SECS - 1), "gr": (n,),
+        "s1s": (n, STEPS), "s1r": (n, STEPS), "ys": (n, STEPS), "yr": (n, STEPS),
+        "s2s": (n, STEPS), "s2r": (n, STEPS), "bs": (n, 2, 3), "br": (n, 2, 2),
+        "gs": (n, 2, 3, SECS - 1), "gr": (n, 2, 3),
     }
     scratch += [sem(shape) for shape in shapes.values()]
     vmem = pl.BlockSpec(memory_space=pltpu.VMEM)

time: 59.5 us -> 56.2 us (0.945)
  Pallas kernels: 57.5 us -> 54.1 us
    pallas_call x1, Pallas kernels: 57.5 us -> 54.1 us  [on_device(): pl.pallas_call(kernel, out_shape=jax.ShapeDtypeStruct((1, TILES, WIDE), f...]
where the time goes in v3:
time: 56.2 us; the launch traced here: 56.1 us
  Pallas kernels  54.1 us (96%)
  local copies, waits for them, and re-layouts  1.97 us (4%)
    pallas_call x1, Pallas kernels, on_device(): pl.pallas_call(kernel, out_shape=jax.ShapeDtypeStruct((1, TILES, WIDE), f...  54.1 us
    unnamed x1, local copies, waits for them, and re-layouts  1.97 us

profile of v3, /device:TPU:1, one launch (start us, length us, event | category | flops | bytes accessed | tf_op | source)
XLA Modules:
  0.0 56.1 jit_solution(4379538284372066041)
XLA Ops:
  0.0 54.1 %shard_map.64 = f32[1,64,2560]{2,1,0:T(8,128)} custom-call(f32[1,64,2560]{2,1,0:T(8,128)} %x_ref.1, f32[64,256,128]{2,1,0:T(8,128)} %bitcast.8, s32[8,64]{1,0:T(8,128)} %bitcast.9, s32[1,64]{1,0:T(1,128)} %bitcast.10, s32[64,64]{1,0:T(8,128)} %land_ref.1, f32[1,40]{1,0:T(1,128)} %bitcast.11), custom_call_target="tpu_custom_call" | custom-call | tf_op jit(solution)/shard_map/pallas_call | solution.py:552
  54.1 2.0 %copy.8 = f32[1,64,2560]{2,1,0:T(8,128)} copy(f32[1,64,2560]{2,1,0:T(8,128)} %shard_map.64) | data formatting | bytes 1310720

commit v4 on v3

--- a/solution.py
+++ b/solution.py
@@ -30,11 +30,11 @@
 
 def kernel(x_ref, w_ref, ids_ref, used_ref, land_ref, coef_ref, out_ref, *scratch):
     n = len(CHUNKS)
-    (wraw, wp, mix, hot, cb, fac, rel) = scratch[:7]
-    (ids, used, land, coef_in, index, idx, wet, coef) = scratch[7:15]
-    per = scratch[15 : 15 + 12 * n]
-    (small, w_sem, own_sem, xs, xr, hs, hr, oss, orr, osl, s1s, s1r, ys, yr, s2s, s2r, bs, br, gs, gr) = (
-        scratch[15 + 12 * n :]
+    (wraw, wp, mix, hot, cb, fac, rel, res) = scratch[:8]
+    (ids, used, land, coef_in, index, idx, wet, coef) = scratch[8:16]
+    per = scratch[16 : 16 + 12 * n]
+    (small, out_sem, w_sem, own_sem, xs, xr, hs, hr, oss, orr, osl, s1s, s1r, ys, yr, s2s, s2r, bs, br, gs, gr) = (
+        scratch[16 + 12 * n :]
     )
     band_in, part, sib, ysum, yrec, flux, oc, ocd, tot, rec, src, given = [
         [per[12 * i + j] for i in range(n)] for j in range(12)
@@ -233,6 +233,9 @@
         src[i][SLOTS] = jnp.zeros((F, 128), f32)
         flat = src[i].reshape((SLOTS + 1) * F, 128)
         spread(band_in[i].at[1], KEEP, F, flat, KEEP)
+        if i + 1 == n:
+            for later in range(1, n):
+                prepare_ocean(later)
         arrivals = to_neighbours(i, band_in[i].at[1])
         arrivals[0].wait_recv()
         spread(band_in[i].at[0], KEEP, F, flat, 0)
@@ -446,21 +449,29 @@
                 x0 = flux[i][pl.ds(8 * g * F + 2 * j, 8, stride=F), :]
                 x1 = flux[i][pl.ds(8 * g * F + 2 * j + 1, 8, stride=F), :]
                 at = pl.ds(starts[i] * CELLS + 128 * j, 128)
-                out_ref[0, pl.ds(8 * g, 8), at] = jnp.where(low, x0, pltpu.roll(x1, CELLS, 1))
-                out_ref[0, pl.ds(PAIRS + 8 * g, 8), at] = jnp.where(
+                res[pl.ds(8 * g, 8), at] = jnp.where(low, x0, pltpu.roll(x1, CELLS, 1))
+                res[pl.ds(PAIRS + 8 * g, 8), at] = jnp.where(
                     low, pltpu.roll(x0, CELLS, 1), x1
                 )
 
-    def finish(i):
-        for g in range(2):
-            for c in back_arrivals(i, g):
-                c.wait_recv()
-        out_ref[0, keep_rows, lanes(i)] = tot[i][1] + rec[i][0] + rec[i][1]
-        out_ref[0, give_rows, lanes(i)] = given[i][0] + given[i][1] + given[i][2]
+    def out_copy(i, g):
+        size = CHUNKS[i] * CELLS // 2
+        at = pl.ds(starts[i] * CELLS + g * size, size)
+        return pltpu.make_async_copy(res.at[:, at], out_ref.at[0, :, at], out_sem.at[i, g])
+
+    def finish(i, g):
+        size = CHUNKS[i] * CELLS // 2
+        at, to = pl.ds(g * size, size), pl.ds(starts[i] * CELLS + g * size, size)
+        for c in back_arrivals(i, g):
+            c.wait_recv()
+        res[keep_rows, to] = tot[i][1, :, at] + rec[i][0, :, at] + rec[i][1, :, at]
+        res[give_rows, to] = given[i][0, :, at] + given[i][1, :, at] + given[i][2, :, at]
+        out_copy(i, g).start()
 
     for i in range(n):
         forward(i)
-        prepare_ocean(i)
+        if i == 0:
+            prepare_ocean(i)
     for i in range(n):
         backward(i)
 
@@ -468,11 +479,14 @@
     def _():
         for i in range(n):
             ocean_out(i)
+            for g in range(2):
+                out_copy(i, g).start()
 
     @pl.when(jnp.logical_not(taker))
     def _():
         for i in range(n):
-            finish(i)
+            for g in range(2):
+                finish(i, g)
 
     for i in range(n):
         for c in to_neighbours(i, band_in[i].at[1]):
@@ -482,6 +496,7 @@
             y_copy(i, q).wait_send()
             flux_copy(i, core, q).wait_send()
         for g in range(2):
+            out_copy(i, g).wait()
             for when, c in back_copies(i, g):
                 pl.when(when)(c.wait_send)
 
@@ -514,6 +529,7 @@
         pltpu.VMEM((TILES * BLOCKS // 2 * top, 128), f32),
         pltpu.VMEM((HALF, 128), f32),
         pltpu.VMEM((HALF * top, 128), f32),
+        pltpu.VMEM((TILES, WIDE), f32),
         pltpu.VMEM((BLOCKS, TILES), jnp.int32),
         pltpu.VMEM((1, TILES), jnp.int32),
         pltpu.VMEM((TILES, CELLS), jnp.int32),
@@ -540,20 +556,19 @@
         ]
     sem = pltpu.SemaphoreType.DMA
     shapes = {
-        "small": (5,), "w": (W_PARTS,), "own": (n,), "xs": (n, 2), "xr": (n, 2),
+        "small": (5,), "out": (n, 2), "w": (W_PARTS,), "own": (n,), "xs": (n, 2), "xr": (n, 2),
         "hs": (n,), "hr": (n, SECS - 1), "oss": (n, SECS - 1, 2), "orr": (n, 2), "osl": (n, 2),
         "s1s": (n, STEPS), "s1r": (n, STEPS), "ys": (n, STEPS), "yr": (n, STEPS),
         "s2s": (n, STEPS), "s2r": (n, STEPS), "bs": (n, 2, 3), "br": (n, 2, 2),
         "gs": (n, 2, 3, SECS - 1), "gr": (n, 2, 3),
     }
     scratch += [sem(shape) for shape in shapes.values()]
-    vmem = pl.BlockSpec(memory_space=pltpu.VMEM)
     anywhere = pl.BlockSpec(memory_space=pl.ANY)
     return pl.pallas_call(
         kernel,
         out_shape=jax.ShapeDtypeStruct((1, TILES, WIDE), f32),
         in_specs=[anywhere] * 6,
-        out_specs=vmem,
+        out_specs=anywhere,
         scratch_shapes=scratch,
         compiler_params=pltpu.CompilerParams(
             collective_id=0, has_side_effects=True, vmem_limit_bytes=56 * 2**20

time: 56.2 us -> 55.6 us (0.989)
  Pallas kernels: 54.1 us -> 53.5 us
    pallas_call x1, Pallas kernels: 54.1 us -> 53.5 us  [on_device(): pl.pallas_call(kernel, out_shape=jax.ShapeDtypeStruct((1, TILES, WIDE), f...]
where the time goes in v4:
time: 55.6 us; the launch traced here: 55.5 us
  Pallas kernels  53.5 us (96%)
  local copies, waits for them, and re-layouts  1.97 us (4%)
    pallas_call x1, Pallas kernels, on_device(): pl.pallas_call(kernel, out_shape=jax.ShapeDtypeStruct((1, TILES, WIDE), f...  53.5 us
    unnamed x1, local copies, waits for them, and re-layouts  1.97 us

profile of v4, /device:TPU:1, one launch (start us, length us, event | category | flops | bytes accessed | tf_op | source)
XLA Modules:
  0.0 55.5 jit_solution(7710576726792942552)
XLA Ops:
  0.0 53.5 %shard_map.64 = f32[1,64,2560]{2,1,0:T(8,128)} custom-call(f32[1,64,2560]{2,1,0:T(8,128)} %x_ref.1, f32[64,256,128]{2,1,0:T(8,128)} %bitcast.8, s32[8,64]{1,0:T(8,128)} %bitcast.9, s32[1,64]{1,0:T(1,128)} %bitcast.10, s32[64,64]{1,0:T(8,128)} %land_ref.1, f32[1,40]{1,0:T(1,128)} %bitcast.11), custom_call_target="tpu_custom_call" | custom-call | tf_op jit(solution)/shard_map/pallas_call | solution.py:567
  53.5 2.0 %copy.8 = f32[1,64,2560]{2,1,0:T(8,128)} copy(f32[1,64,2560]{2,1,0:T(8,128)} %shard_map.64) | data formatting | bytes 1310720

commit v5 on v4

--- a/solution.py
+++ b/solution.py
@@ -170,14 +170,14 @@
         w_copy[i].wait()
         lax.fori_loop(i * per_w, (i + 1) * per_w, prepare, 0, unroll=4)
 
-    take_over(0)
-
     @pl.when(taker)
     def _():
         for i in range(n):
             for who in range(SECS - 1):
                 for z in range(2):
                     ocean_to(i, who, z).start()
+
+    take_over(0)
 
     for c in tables:
         c.wait()

time: 55.6 us -> 55.6 us (level)
  no operation moved by 1% of the time
where the time goes in v5:
time: 55.6 us; the launch traced here: 55.5 us
  Pallas kernels  53.5 us (96%)
  local copies, waits for them, and re-layouts  1.97 us (4%)
    pallas_call x1, Pallas kernels, on_device(): pl.pallas_call(kernel, out_shape=jax.ShapeDtypeStruct((1, TILES, WIDE), f...  53.5 us
    unnamed x1, local copies, waits for them, and re-layouts  1.97 us

profile of v5, /device:TPU:1, one launch (start us, length us, event | category | flops | bytes accessed | tf_op | source)
XLA Modules:
  0.0 55.5 jit_solution(17094670847978471777)
XLA Ops:
  0.0 53.5 %shard_map.64 = f32[1,64,2560]{2,1,0:T(8,128)} custom-call(f32[1,64,2560]{2,1,0:T(8,128)} %x_ref.1, f32[64,256,128]{2,1,0:T(8,128)} %bitcast.8, s32[8,64]{1,0:T(8,128)} %bitcast.9, s32[1,64]{1,0:T(1,128)} %bitcast.10, s32[64,64]{1,0:T(8,128)} %land_ref.1, f32[1,40]{1,0:T(1,128)} %bitcast.11), custom_call_target="tpu_custom_call" | custom-call | tf_op jit(solution)/shard_map/pallas_call | solution.py:567
  53.5 2.0 %copy.8 = f32[1,64,2560]{2,1,0:T(8,128)} copy(f32[1,64,2560]{2,1,0:T(8,128)} %shard_map.64) | data formatting | bytes 1310720
